TPU v7x, 512 devices: a whole 4x4x16 slice. The times are simulated.
512 devices in a mesh: inner: 64 (over y, z_lo, core), outer: 8 (over z_hi, x).
Axes of the slice: x: 4, y: 4, z: 16 (z_hi: 2, z_lo: 8; z = z_hi * 8 + z_lo), core: 2. Of those that a mesh axis runs over, the one named last changes fastest.
Arguments:
- grads: float32 [64, 8, 128, 8192], P('inner', 'outer'), may hold values from -0.875 to 0.875
- first_exponents: int32 [64, 8, 128, 64], P('inner', 'outer'), may hold values from -13 to -9
- second_exponents: int32 [8, 128, 64], P('outer', None, 'inner'), may hold values from -11 to -6
Outputs:
- reduced: float32 [128, 8192], P('outer', 'inner')
All inputs are finite; a program needn't handle non-finite values.
Results may differ from a plain program's by a relative error of at most 0.01.
Values may be sent and summed in bfloat16 or wider, within the bound.
A program may use at most 64 MiB of HBM per device.

v0:
```python
import math

import jax
import jax.numpy as jnp
from jax import lax
from jax.experimental import pallas as pl
from jax.experimental.pallas import tpu as pltpu
from jax.sharding import PartitionSpec as P

SATURATION = 448.0
RSQRT = 1.0 / math.sqrt(128.0)
LOGICAL = pl.DeviceIdType.MESH
F32 = jnp.float32
BF16 = jnp.bfloat16
CHUNKS = 8
CHUNK_ROWS = 128 // CHUNKS
OWNERS = CHUNK_ROWS // 16
GROUP = 512 // CHUNK_ROWS
ORDER = tuple(
    (item[0], int(item[1:]))
    for line in (
        "e0 a0 e1 a1", "e2 a2 e3 a3", "l0 e4 a4 e5", "a5 m0 e6 a6", "m1 e7 a7 m2",
        "m3 m4 m5 n0", "n1 m6 n2 m7", "n3 n4 r0 n5", "r1 n6 r2 n7", "r3 r4 r5 s0",
        "r6 s1 r7 s2", "s3 s4 s5 s6", "s7",
    )
    for item in line.split()
)


def sign_table():
    row = lax.broadcasted_iota(jnp.int32, (256, 256), 0)
    col = lax.broadcasted_iota(jnp.int32, (256, 256), 1)
    shared = row & col & 127
    shared = shared ^ (shared >> 4)
    shared = shared ^ (shared >> 2)
    shared = shared ^ (shared >> 1)
    signs = (1 - 2 * (shared & 1)).astype(F32)
    return jnp.where((row // 128) == (col // 128), signs, 0.0).astype(BF16)


def limits(exponents):
    return jnp.left_shift(1, exponents + 13).astype(F32) * F32(SATURATION / 8192.0)


def clip(value, bound):
    return jnp.minimum(jnp.maximum(value, -bound), bound)


def kernel(
    grads_ref, first_ref, second_ref, out_ref,
    gbuf, first_buf, second_buf, table, lim1, lim2, enc, arecv,
    y1send, y1recv, y2send, y2recv, z1send, z1own, z1recv, fsend, frecv, limrecv,
    load_sem, scale_sem, send_sem, a_rsem, y1_rsem, y2_rsem, z1_rsem, l_rsem, f_rsem,
):
    inner = lax.axis_index("inner")
    outer = lax.axis_index("outer")
    core = inner % 2
    z = (inner // 2) % 8
    y = inner // 16
    run, role = z // 4, z % 4
    y_right, y_left, y_far = (y + 1) % 4, (y + 3) % 4, (y + 2) % 4

    def inner_of(yy, zz, cc):
        return (yy * 8 + zz) * 2 + cc

    sibling = inner_of(y, z, 1 - core)
    right = inner_of(y_right, z, core)
    left = inner_of(y_left, z, core)
    across = inner_of(y, (1 - run) * 4 + role, core)
    mates = [inner_of(y, run * 4 + (role + d) % 4, core) for d in (1, 2, 3)]

    def remote(src, dst, stage, rsem, i, o=None):
        return pltpu.make_async_remote_copy(
            src_ref=src, dst_ref=dst, send_sem=send_sem.at[stage], recv_sem=rsem,
            device_id=(i, outer if o is None else o), device_id_type=LOGICAL,
        )

    def wait_recv(dst, rsem):
        remote(dst, dst, 0, rsem, sibling).wait_recv()

    def wait_send(like, stage):
        remote(like, like, stage, f_rsem.at[0], sibling).wait_send()

    scale_loads = [
        pltpu.make_async_copy(first_ref, first_buf, scale_sem.at[0]),
        pltpu.make_async_copy(second_ref, second_buf, scale_sem.at[1]),
    ]
    loads = [
        pltpu.make_async_copy(
            grads_ref.at[pl.ds(q * CHUNK_ROWS, CHUNK_ROWS)], gbuf.at[q], load_sem.at[q]
        )
        for q in range(CHUNKS)
    ]
    for load in scale_loads + loads:
        load.start()

    barrier = pltpu.get_barrier_semaphore()
    partners = [sibling, right, left, across] + mates
    for i in partners:
        pl.semaphore_signal(barrier, inc=1, device_id=(i, outer), device_id_type=LOGICAL)
    for d in range(1, 8):
        for i in (inner, across):
            pl.semaphore_signal(
                barrier, inc=1, device_id=(i, (outer + d) % 8), device_id_type=LOGICAL
            )

    table[...] = sign_table()
    for load in scale_loads:
        load.wait()
    first = limits(first_buf[...])
    lim1[...] = jnp.concatenate([first, first], axis=0).T.astype(BF16)
    second = jnp.broadcast_to(limits(second_buf[...]), (128, 128)).T.astype(BF16)
    for owner in range(8):
        lim2[owner] = second[owner * 16 : (owner + 1) * 16]
    limrecv[outer] = lim2[outer]

    def encode(q):
        loads[q].wait()
        weights = table[...]
        rows = slice(q * CHUNK_ROWS, (q + 1) * CHUNK_ROWS)
        for base in range(0, 32, GROUP):
            lhs = jnp.concatenate(
                [
                    gbuf[q, :, (base + k) * 256 : (base + k + 1) * 256].astype(BF16)
                    for k in range(GROUP)
                ],
                axis=0,
            )
            rotated = jnp.dot(lhs, weights, preferred_element_type=F32) * F32(RSQRT)
            rotated = rotated.astype(BF16)
            for k in range(GROUP):
                pair = base + k
                for c in range(2):
                    block = 2 * pair + c
                    bound = jnp.broadcast_to(lim1[rows, block : block + 1], (CHUNK_ROWS, 128))
                    value = rotated[k * CHUNK_ROWS : (k + 1) * CHUNK_ROWS, c * 128 : (c + 1) * 128]
                    enc[q, c, pair // 8, pair % 8 // 4, pair % 4] = clip(value, bound)

    def pair_send(q):
        remote(enc.at[q, 1 - core], arecv.at[q], 0, a_rsem.at[q], sibling).start()

    def pair_sum(q, yy, half):
        return enc[q, core, yy, half] + arecv[q, yy, half]

    def limit_send(q):
        for d in range(1, 8):
            owner = (outer + d) % 8
            remote(lim2.at[owner], limrecv.at[outer], 4, l_rsem.at[0], inner, owner).start()

    def ring_one(q):
        wait_recv(arecv.at[q], a_rsem.at[q])
        for way, to in ((0, right), (1, left)):
            y1send[q, way] = pair_sum(q, y_far, way)
            remote(y1send.at[q, way], y1recv.at[q, way], 1, y1_rsem.at[q], to).start()
        for way, near, to in ((0, y_right, right), (1, y_left, left)):
            y2send[q, way, 0] = pair_sum(q, near, 1 - way)
            remote(y2send.at[q, way, 0], y2recv.at[q, way, 0], 2, y2_rsem.at[q], to).start()

    def ring_two(q):
        wait_recv(y1recv.at[q], y1_rsem.at[q])
        for way, near, to in ((0, y_right, right), (1, y_left, left)):
            value = enc[q, core, near, way].astype(F32) + arecv[q, near, way].astype(F32)
            y2send[q, way, 1] = (value + y1recv[q, way].astype(F32)).astype(BF16)
            remote(y2send.at[q, way, 1], y2recv.at[q, way, 1], 2, y2_rsem.at[q], to).start()

    def run_one(q):
        wait_recv(y2recv.at[q], y2_rsem.at[q])
        for d in (1, 2, 3, 0):
            r = (role + d) % 4
            for half in range(2):
                value = enc[q, core, y, half, r].astype(F32) + arecv[q, y, half, r].astype(F32)
                value = value + y2recv[q, half, 1, r].astype(F32) + y2recv[q, 1 - half, 0, r].astype(F32)
                if d:
                    z1send[q, d - 1, half] = value.astype(BF16)
                else:
                    z1own[q, half] = value
            if d:
                remote(z1send.at[q, d - 1], z1recv.at[q, d - 1], 3, z1_rsem.at[q], mates[d - 1]).start()

    def run_two(q):
        wait_recv(z1recv.at[q], z1_rsem.at[q])
        for half in range(2):
            value = z1own[q, half]
            for d in range(3):
                value = value + z1recv[q, d, half].astype(F32)
            for h in range(OWNERS):
                owner = OWNERS * q + h
                fsend[half, owner] = value[h * 16 : (h + 1) * 16].astype(BF16)
                here = jnp.logical_and(owner == outer, half == run)

                @pl.when(jnp.logical_not(here))
                def _():
                    remote(
                        fsend.at[half, owner], frecv.at[8 * run + outer], 5, f_rsem.at[0],
                        inner_of(y, 4 * half + role, core), owner,
                    ).start()

    stages = {
        "e": encode, "a": pair_send, "l": limit_send, "m": ring_one, "n": ring_two,
        "r": run_one, "s": run_two,
    }
    for name, q in ORDER:
        if name == "a" and q == 0:
            pl.semaphore_wait(barrier, len(partners) + 14)
        stages[name](q)

    frecv[8 * run + outer] = fsend[run, outer]
    for stage, like in enumerate(
        (arecv, y1send, y2send, z1send, lim2.at[pl.ds(0, 7)], frecv.at[pl.ds(0, 15)])
    ):
        wait_send(like, stage)
    wait_recv(limrecv.at[pl.ds(0, 7)], l_rsem.at[0])
    wait_recv(frecv.at[pl.ds(0, 15)], f_rsem.at[0])
    total = jnp.zeros((16, 128), F32)
    for group in range(8):
        value = frecv[group].astype(F32) + frecv[8 + group].astype(F32)
        total = total + clip(value, limrecv[group].astype(F32))
    high = total.astype(BF16)
    low = (total - high.astype(F32)).astype(BF16)
    signs = table[0:128, 0:128]
    result = jnp.dot(high, signs, preferred_element_type=F32)
    result = result + jnp.dot(low, signs, preferred_element_type=F32)
    out_ref[...] = result * F32(RSQRT)


def shards(grads, first_exponents, second_exponents):
    rows, columns = grads.shape[2], grads.shape[3]
    first = first_exponents.reshape(rows, columns // 128).T
    second = second_exponents.reshape(1, rows)
    operands = (grads.reshape(rows, columns), first, second)
    dma = pltpu.SemaphoreType.DMA
    c, r = CHUNKS, CHUNK_ROWS
    return pl.pallas_call(
        kernel,
        out_shape=jax.ShapeDtypeStruct((16, 128), F32),
        in_specs=[pl.BlockSpec(memory_space=pltpu.HBM)] * 3,
        out_specs=pl.BlockSpec(memory_space=pltpu.VMEM),
        scratch_shapes=[
            pltpu.VMEM((c, r, columns), F32),
            pltpu.VMEM((columns // 128, rows), jnp.int32),
            pltpu.VMEM((1, rows), jnp.int32),
            pltpu.VMEM((256, 256), BF16),
            pltpu.VMEM((128, 128), BF16),
            pltpu.VMEM((8, 16, 128), BF16),
            pltpu.VMEM((c, 2, 4, 2, 4, r, 128), BF16),
            pltpu.VMEM((c, 4, 2, 4, r, 128), BF16),
            pltpu.VMEM((c, 2, 4, r, 128), BF16),
            pltpu.VMEM((c, 2, 4, r, 128), BF16),
            pltpu.VMEM((c, 2, 2, 4, r, 128), BF16),
            pltpu.VMEM((c, 2, 2, 4, r, 128), BF16),
            pltpu.VMEM((c, 3, 2, r, 128), BF16),
            pltpu.VMEM((c, 2, r, 128), F32),
            pltpu.VMEM((c, 3, 2, r, 128), BF16),
            pltpu.VMEM((2, 8, 16, 128), BF16),
            pltpu.VMEM((16, 16, 128), BF16),
            pltpu.VMEM((8, 16, 128), BF16),
            dma((c,)),
            dma((2,)),
            dma((6,)),
            dma((c,)),
            dma((c,)),
            dma((c,)),
            dma((c,)),
            dma((1,)),
            dma((1,)),
        ],
        compiler_params=pltpu.CompilerParams(
            collective_id=0, has_side_effects=True, vmem_limit_bytes=48 * 1024 * 1024
        ),
        name="reduce_scatter",
    )(*(pltpu.with_memory_space_constraint(x, pltpu.HBM) for x in operands))


def solution(mesh):
    placed = (
        P("inner", "outer", None, None),
        P("inner", "outer", None, None),
        P("outer", None, "inner"),
    )
    return jax.shard_map(
        shards, mesh=mesh, in_specs=placed, out_specs=P("outer", "inner"), check_vma=False
    )
```

profile of v0, /device:TPU:6, one launch (start us, length us, event | category | flops | bytes accessed | tf_op | source)
XLA Modules:
  0.0 39.9 jit_solution(15435493803739253669)
XLA Ops:
  0.0 39.3 %reduce_scatter.1 = f32[16,128]{1,0:T(8,128)S(1)} custom-call(f32[128,8192]{1,0:T(8,128)} %bitcast.5, s32[64,128]{1,0:T(8,128)} %bitcast.6, s32[1,128]{1,0:T(1,128)} %bitcast.7), custom_call_target="tpu_custom_call" | custom-call | tf_op jit(solution)/shard_map/reduce_scatter/pallas_call | solution.py:233
  39.3 0.6 %copy.5 = f32[16,128]{1,0:T(8,128)} copy(f32[16,128]{1,0:T(8,128)S(1)} %reduce_scatter.1) | data formatting | bytes 16384
where the time goes:
time: 40 us; the launch traced here: 39.9 us
  Pallas kernels  39.3 us (98%)
  local copies, waits for them, and re-layouts  0.6 us (2%)
    pallas_call x1, Pallas kernels, shards(): pl.pallas_call(kernel, out_shape=jax.ShapeDtypeStruct((16, 128), F32), in...  39.3 us

commit v1 on v0

--- a/solution.py
+++ b/solution.py
@@ -12,16 +12,14 @@
 LOGICAL = pl.DeviceIdType.MESH
 F32 = jnp.float32
 BF16 = jnp.bfloat16
-CHUNKS = 8
+CHUNKS = 4
 CHUNK_ROWS = 128 // CHUNKS
 OWNERS = CHUNK_ROWS // 16
-GROUP = 512 // CHUNK_ROWS
 ORDER = tuple(
     (item[0], int(item[1:]))
     for line in (
-        "e0 a0 e1 a1", "e2 a2 e3 a3", "l0 e4 a4 e5", "a5 m0 e6 a6", "m1 e7 a7 m2",
-        "m3 m4 m5 n0", "n1 m6 n2 m7", "n3 n4 r0 n5", "r1 n6 r2 n7", "r3 r4 r5 s0",
-        "r6 s1 r7 s2", "s3 s4 s5 s6", "s7",
+        "f0 f1 f2 h0", "f3 h1 l0 m0", "m1 h2 m2 h3", "m3 o0 k0 o1", "n0 k1 n1 k2",
+        "o2 n2 k3 n3", "o3 r0 r1 r2", "r3 s0 s1 s2", "s3",
     )
     for item in line.split()
 )
@@ -85,14 +83,21 @@
         pltpu.make_async_copy(first_ref, first_buf, scale_sem.at[0]),
         pltpu.make_async_copy(second_ref, second_buf, scale_sem.at[1]),
     ]
-    loads = [
-        pltpu.make_async_copy(
-            grads_ref.at[pl.ds(q * CHUNK_ROWS, CHUNK_ROWS)], gbuf.at[q], load_sem.at[q]
-        )
-        for q in range(CHUNKS)
-    ]
-    for load in scale_loads + loads:
-        load.start()
+    places = (y_far, y_right, y_left, y)
+    parts = {"f": (0,), "h": (1, 2), "o": (3,)}
+
+    def load(q, d):
+        columns = pl.ds(pl.multiple_of(places[d] * 2048, 2048), 2048)
+        return pltpu.make_async_copy(
+            grads_ref.at[pl.ds(q * CHUNK_ROWS, CHUNK_ROWS), columns], gbuf.at[q, d], load_sem.at[q, d]
+        )
+
+    for copy in scale_loads:
+        copy.start()
+    for part in parts.values():
+        for q in range(CHUNKS):
+            for d in part:
+                load(q, d).start()
 
     barrier = pltpu.get_barrier_semaphore()
     partners = [sibling, right, left, across] + mates
@@ -105,70 +110,84 @@
             )
 
     table[...] = sign_table()
-    for load in scale_loads:
-        load.wait()
-    first = limits(first_buf[...])
-    lim1[...] = jnp.concatenate([first, first], axis=0).T.astype(BF16)
+    for copy in scale_loads:
+        copy.wait()
+    first = jnp.concatenate(
+        [first_buf[pl.ds(pl.multiple_of(place * 16, 16), 16), :] for place in places] * 2, axis=0
+    )
+    lim1[...] = limits(first).T.astype(BF16)
     second = jnp.broadcast_to(limits(second_buf[...]), (128, 128)).T.astype(BF16)
     for owner in range(8):
         lim2[owner] = second[owner * 16 : (owner + 1) * 16]
     limrecv[outer] = lim2[outer]
 
-    def encode(q):
-        loads[q].wait()
-        weights = table[...]
+    def encode(q, part):
         rows = slice(q * CHUNK_ROWS, (q + 1) * CHUNK_ROWS)
-        for base in range(0, 32, GROUP):
-            lhs = jnp.concatenate(
-                [
-                    gbuf[q, :, (base + k) * 256 : (base + k + 1) * 256].astype(BF16)
-                    for k in range(GROUP)
-                ],
-                axis=0,
-            )
-            rotated = jnp.dot(lhs, weights, preferred_element_type=F32) * F32(RSQRT)
-            rotated = rotated.astype(BF16)
-            for k in range(GROUP):
-                pair = base + k
-                for c in range(2):
-                    block = 2 * pair + c
-                    bound = jnp.broadcast_to(lim1[rows, block : block + 1], (CHUNK_ROWS, 128))
-                    value = rotated[k * CHUNK_ROWS : (k + 1) * CHUNK_ROWS, c * 128 : (c + 1) * 128]
-                    enc[q, c, pair // 8, pair % 8 // 4, pair % 4] = clip(value, bound)
-
-    def pair_send(q):
-        remote(enc.at[q, 1 - core], arecv.at[q], 0, a_rsem.at[q], sibling).start()
-
-    def pair_sum(q, yy, half):
-        return enc[q, core, yy, half] + arecv[q, yy, half]
+        pairs = [(d, k) for d in parts[part] for k in range(8)]
+        for d in parts[part]:
+            load(q, d).wait()
+        lhs = jnp.concatenate(
+            [gbuf[q, d, :, k * 256 : (k + 1) * 256].astype(BF16) for d, k in pairs], axis=0
+        )
+        rotated = jnp.dot(lhs, table[...], preferred_element_type=F32) * F32(RSQRT)
+        rotated = rotated.astype(BF16)
+        for i, (d, k) in enumerate(pairs):
+            for c in range(2):
+                lane = 16 * d + 2 * k + c
+                bound = jnp.broadcast_to(lim1[rows, lane : lane + 1], (CHUNK_ROWS, 128))
+                value = rotated[i * CHUNK_ROWS : (i + 1) * CHUNK_ROWS, c * 128 : (c + 1) * 128]
+                enc[q, c, d, k // 4, k % 4] = clip(value, bound)
+
+    def part_copy(q, part):
+        span = pl.ds(parts[part][0], len(parts[part]))
+        return remote(
+            enc.at[q, 1 - core, span], arecv.at[q, span], 0,
+            a_rsem.at[q, parts[part][0]], sibling,
+        )
+
+    def encode_send(part):
+        def stage(q):
+            encode(q, part)
+            if part == "f" and q == 0:
+                pl.semaphore_wait(barrier, len(partners) + 14)
+            part_copy(q, part).start()
+
+        return stage
+
+    def pair_sum(q, d, half):
+        return enc[q, core, d, half] + arecv[q, d, half]
 
     def limit_send(q):
         for d in range(1, 8):
             owner = (outer + d) % 8
             remote(lim2.at[owner], limrecv.at[outer], 4, l_rsem.at[0], inner, owner).start()
 
-    def ring_one(q):
-        wait_recv(arecv.at[q], a_rsem.at[q])
+    def ring_far(q):
+        part_copy(q, "f").wait_recv()
         for way, to in ((0, right), (1, left)):
-            y1send[q, way] = pair_sum(q, y_far, way)
+            y1send[q, way] = pair_sum(q, 0, way)
             remote(y1send.at[q, way], y1recv.at[q, way], 1, y1_rsem.at[q], to).start()
-        for way, near, to in ((0, y_right, right), (1, y_left, left)):
-            y2send[q, way, 0] = pair_sum(q, near, 1 - way)
+
+    def ring_near(q):
+        part_copy(q, "h").wait_recv()
+        for way, to in ((0, right), (1, left)):
+            y2send[q, way, 0] = pair_sum(q, 1 + way, 1 - way)
             remote(y2send.at[q, way, 0], y2recv.at[q, way, 0], 2, y2_rsem.at[q], to).start()
 
-    def ring_two(q):
+    def ring_on(q):
         wait_recv(y1recv.at[q], y1_rsem.at[q])
-        for way, near, to in ((0, y_right, right), (1, y_left, left)):
-            value = enc[q, core, near, way].astype(F32) + arecv[q, near, way].astype(F32)
+        for way, to in ((0, right), (1, left)):
+            value = enc[q, core, 1 + way, way].astype(F32) + arecv[q, 1 + way, way].astype(F32)
             y2send[q, way, 1] = (value + y1recv[q, way].astype(F32)).astype(BF16)
             remote(y2send.at[q, way, 1], y2recv.at[q, way, 1], 2, y2_rsem.at[q], to).start()
 
     def run_one(q):
+        part_copy(q, "o").wait_recv()
         wait_recv(y2recv.at[q], y2_rsem.at[q])
         for d in (1, 2, 3, 0):
             r = (role + d) % 4
             for half in range(2):
-                value = enc[q, core, y, half, r].astype(F32) + arecv[q, y, half, r].astype(F32)
+                value = enc[q, core, 3, half, r].astype(F32) + arecv[q, 3, half, r].astype(F32)
                 value = value + y2recv[q, half, 1, r].astype(F32) + y2recv[q, 1 - half, 0, r].astype(F32)
                 if d:
                     z1send[q, d - 1, half] = value.astype(BF16)
@@ -195,13 +214,9 @@
                         inner_of(y, 4 * half + role, core), owner,
                     ).start()
 
-    stages = {
-        "e": encode, "a": pair_send, "l": limit_send, "m": ring_one, "n": ring_two,
-        "r": run_one, "s": run_two,
-    }
+    stages = {part: encode_send(part) for part in parts}
+    stages.update(l=limit_send, m=ring_far, k=ring_near, n=ring_on, r=run_one, s=run_two)
     for name, q in ORDER:
-        if name == "a" and q == 0:
-            pl.semaphore_wait(barrier, len(partners) + 14)
         stages[name](q)
 
     frecv[8 * run + outer] = fsend[run, outer]
@@ -236,7 +251,7 @@
         in_specs=[pl.BlockSpec(memory_space=pltpu.HBM)] * 3,
         out_specs=pl.BlockSpec(memory_space=pltpu.VMEM),
         scratch_shapes=[
-            pltpu.VMEM((c, r, columns), F32),
+            pltpu.VMEM((c, 4, r, columns // 4), F32),
             pltpu.VMEM((columns // 128, rows), jnp.int32),
             pltpu.VMEM((1, rows), jnp.int32),
             pltpu.VMEM((256, 256), BF16),
@@ -254,10 +269,10 @@
             pltpu.VMEM((2, 8, 16, 128), BF16),
             pltpu.VMEM((16, 16, 128), BF16),
             pltpu.VMEM((8, 16, 128), BF16),
-            dma((c,)),
+            dma((c, 4)),
             dma((2,)),
             dma((6,)),
-            dma((c,)),
+            dma((c, 4)),
             dma((c,)),
             dma((c,)),
             dma((c,)),

time: 40 us -> 38.5 us (0.963)
  the two profiles are of different devices: /device:TPU:6 before, /device:TPU:38 now
where the time goes in v1:
time: 38.5 us; the launch traced here: 38.4 us
  Pallas kernels  37.8 us (98%)
  local copies, waits for them, and re-layouts  0.6 us (2%)
    pallas_call x1, Pallas kernels, shards(): pl.pallas_call(kernel, out_shape=jax.ShapeDtypeStruct((16, 128), F32), in...  37.8 us

profile of v1, /device:TPU:38, one launch (start us, length us, event | category | flops | bytes accessed | tf_op | source)
XLA Modules:
  0.0 38.4 jit_solution(5780228731793533325)
XLA Ops:
  0.0 37.8 %reduce_scatter.1 = f32[16,128]{1,0:T(8,128)S(1)} custom-call(f32[128,8192]{1,0:T(8,128)} %bitcast.5, s32[64,128]{1,0:T(8,128)} %bitcast.6, s32[1,128]{1,0:T(1,128)} %bitcast.7), custom_call_target="tpu_custom_call" | custom-call | tf_op jit(solution)/shard_map/reduce_scatter/pallas_call | solution.py:248
  37.8 0.6 %copy.5 = f32[16,128]{1,0:T(8,128)} copy(f32[16,128]{1,0:T(8,128)S(1)} %reduce_scatter.1) | data formatting | bytes 16384

commit v2 on v1

--- a/solution.py
+++ b/solution.py
@@ -13,13 +13,12 @@
 F32 = jnp.float32
 BF16 = jnp.bfloat16
 CHUNKS = 4
-CHUNK_ROWS = 128 // CHUNKS
-OWNERS = CHUNK_ROWS // 16
+CHUNK_ROWS = 64
 ORDER = tuple(
     (item[0], int(item[1:]))
     for line in (
-        "f0 f1 f2 h0", "f3 h1 l0 m0", "m1 h2 m2 h3", "m3 o0 k0 o1", "n0 k1 n1 k2",
-        "o2 n2 k3 n3", "o3 r0 r1 r2", "r3 s0 s1 s2", "s3",
+        "f0 h0 f1 o0", "f2 h1 m0 m1", "h2 k0 m2 f3", "h3 o1 n0 k1", "n1 m3 o2 o3",
+        "k2 n2 k3 r0", "r1 n3 r2 l0", "s0 r3 s1 s2", "s3",
     )
     for item in line.split()
 )
@@ -86,29 +85,59 @@
     places = (y_far, y_right, y_left, y)
     parts = {"f": (0,), "h": (1, 2), "o": (3,)}
 
+    def rows_of(q):
+        return pl.ds(q // 2 * CHUNK_ROWS, CHUNK_ROWS)
+
     def load(q, d):
-        columns = pl.ds(pl.multiple_of(places[d] * 2048, 2048), 2048)
+        columns = pl.ds(pl.multiple_of(places[d] * 2048 + q % 2 * 1024, 1024), 1024)
         return pltpu.make_async_copy(
-            grads_ref.at[pl.ds(q * CHUNK_ROWS, CHUNK_ROWS), columns], gbuf.at[q, d], load_sem.at[q, d]
+            grads_ref.at[rows_of(q), columns], gbuf.at[q, d], load_sem.at[q, d]
         )
+
+    def start_loads(q):
+        for d in range(4):
+            load(q, d).start()
 
     for copy in scale_loads:
         copy.start()
-    for part in parts.values():
-        for q in range(CHUNKS):
-            for d in part:
-                load(q, d).start()
-
+    start_loads(0)
+
+    lower, first_run = 1 - outer // 4, 1 - run
+    klass = lower * first_run
     barrier = pltpu.get_barrier_semaphore()
-    partners = [sibling, right, left, across] + mates
-    for i in partners:
-        pl.semaphore_signal(barrier, inc=1, device_id=(i, outer), device_id_type=LOGICAL)
-    for d in range(1, 8):
-        for i in (inner, across):
-            pl.semaphore_signal(
-                barrier, inc=1, device_id=(i, (outer + d) % 8), device_id_type=LOGICAL
-            )
-
+
+    def hello(i, o):
+        pl.semaphore_signal(barrier, inc=1, device_id=(i, o), device_id_type=LOGICAL)
+
+    def hello_outer(same):
+        for d in range(1, 8):
+            owner = (outer + d) % 8
+            other_lower = 1 - owner // 4
+            for i, other in ((inner, other_lower * first_run), (across, other_lower * run)):
+
+                @pl.when((other == klass) if same else (other != klass))
+                def _():
+                    hello(i, owner)
+
+        @pl.when((lower * run == klass) if same else (lower * run != klass))
+        def _():
+            hello(across, outer)
+
+    def enter():
+        pl.semaphore_wait(barrier, 21 - 12 * klass)
+        hello_outer(False)
+
+    def enter_outer():
+        @pl.when(klass == 1)
+        def _():
+            pl.semaphore_wait(barrier, 12)
+
+    for i in [sibling, right, left] + mates:
+        hello(i, outer)
+    hello_outer(True)
+
+    for q in range(1, CHUNKS):
+        start_loads(q)
     table[...] = sign_table()
     for copy in scale_loads:
         copy.wait()
@@ -122,8 +151,8 @@
     limrecv[outer] = lim2[outer]
 
     def encode(q, part):
-        rows = slice(q * CHUNK_ROWS, (q + 1) * CHUNK_ROWS)
-        pairs = [(d, k) for d in parts[part] for k in range(8)]
+        bounds = lim1[rows_of(q), :]
+        pairs = [(d, k) for d in parts[part] for k in range(4)]
         for d in parts[part]:
             load(q, d).wait()
         lhs = jnp.concatenate(
@@ -133,10 +162,10 @@
         rotated = rotated.astype(BF16)
         for i, (d, k) in enumerate(pairs):
             for c in range(2):
-                lane = 16 * d + 2 * k + c
-                bound = jnp.broadcast_to(lim1[rows, lane : lane + 1], (CHUNK_ROWS, 128))
+                lane = 16 * d + 8 * (q % 2) + 2 * k + c
+                bound = jnp.broadcast_to(bounds[:, lane : lane + 1], (CHUNK_ROWS, 128))
                 value = rotated[i * CHUNK_ROWS : (i + 1) * CHUNK_ROWS, c * 128 : (c + 1) * 128]
-                enc[q, c, d, k // 4, k % 4] = clip(value, bound)
+                enc[q, c, d, k] = clip(value, bound)
 
     def part_copy(q, part):
         span = pl.ds(parts[part][0], len(parts[part]))
@@ -149,15 +178,17 @@
         def stage(q):
             encode(q, part)
             if part == "f" and q == 0:
-                pl.semaphore_wait(barrier, len(partners) + 14)
+                enter()
             part_copy(q, part).start()
 
         return stage
 
-    def pair_sum(q, d, half):
-        return enc[q, core, d, half] + arecv[q, d, half]
+    def pair_sum(q, d, way):
+        two = pl.ds(2 * way, 2)
+        return enc[q, core, d, two] + arecv[q, d, two]
 
     def limit_send(q):
+        enter_outer()
         for d in range(1, 8):
             owner = (outer + d) % 8
             remote(lim2.at[owner], limrecv.at[outer], 4, l_rsem.at[0], inner, owner).start()
@@ -177,7 +208,8 @@
     def ring_on(q):
         wait_recv(y1recv.at[q], y1_rsem.at[q])
         for way, to in ((0, right), (1, left)):
-            value = enc[q, core, 1 + way, way].astype(F32) + arecv[q, 1 + way, way].astype(F32)
+            two = pl.ds(2 * way, 2)
+            value = enc[q, core, 1 + way, two].astype(F32) + arecv[q, 1 + way, two].astype(F32)
             y2send[q, way, 1] = (value + y1recv[q, way].astype(F32)).astype(BF16)
             remote(y2send.at[q, way, 1], y2recv.at[q, way, 1], 2, y2_rsem.at[q], to).start()
 
@@ -186,33 +218,34 @@
         wait_recv(y2recv.at[q], y2_rsem.at[q])
         for d in (1, 2, 3, 0):
             r = (role + d) % 4
-            for half in range(2):
-                value = enc[q, core, 3, half, r].astype(F32) + arecv[q, 3, half, r].astype(F32)
-                value = value + y2recv[q, half, 1, r].astype(F32) + y2recv[q, 1 - half, 0, r].astype(F32)
-                if d:
-                    z1send[q, d - 1, half] = value.astype(BF16)
-                else:
-                    z1own[q, half] = value
+            way, place = r // 2, r % 2
+            value = enc[q, core, 3, r].astype(F32) + arecv[q, 3, r].astype(F32)
+            value = value + y2recv[q, way, 1, place].astype(F32)
+            value = value + y2recv[q, 1 - way, 0, place].astype(F32)
             if d:
+                z1send[q, d - 1] = value.astype(BF16)
                 remote(z1send.at[q, d - 1], z1recv.at[q, d - 1], 3, z1_rsem.at[q], mates[d - 1]).start()
+            else:
+                z1own[q] = value
 
     def run_two(q):
         wait_recv(z1recv.at[q], z1_rsem.at[q])
-        for half in range(2):
-            value = z1own[q, half]
-            for d in range(3):
-                value = value + z1recv[q, d, half].astype(F32)
-            for h in range(OWNERS):
-                owner = OWNERS * q + h
-                fsend[half, owner] = value[h * 16 : (h + 1) * 16].astype(BF16)
-                here = jnp.logical_and(owner == outer, half == run)
-
-                @pl.when(jnp.logical_not(here))
-                def _():
-                    remote(
-                        fsend.at[half, owner], frecv.at[8 * run + outer], 5, f_rsem.at[0],
-                        inner_of(y, 4 * half + role, core), owner,
-                    ).start()
+        value = z1own[q]
+        for d in range(3):
+            value = value + z1recv[q, d].astype(F32)
+        value = value.astype(BF16)
+        half = q % 2
+        for h in range(4):
+            owner = q // 2 * 4 + h
+            fsend[half, owner] = value[h * 16 : (h + 1) * 16]
+            here = jnp.logical_and(owner == outer, half == run)
+
+            @pl.when(jnp.logical_not(here))
+            def _():
+                remote(
+                    fsend.at[half, owner], frecv.at[8 * run + outer], 5, f_rsem.at[0],
+                    inner_of(y, 4 * half + role, core), owner,
+                ).start()
 
     stages = {part: encode_send(part) for part in parts}
     stages.update(l=limit_send, m=ring_far, k=ring_near, n=ring_on, r=run_one, s=run_two)
@@ -251,21 +284,21 @@
         in_specs=[pl.BlockSpec(memory_space=pltpu.HBM)] * 3,
         out_specs=pl.BlockSpec(memory_space=pltpu.VMEM),
         scratch_shapes=[
-            pltpu.VMEM((c, 4, r, columns // 4), F32),
+            pltpu.VMEM((c, 4, r, 1024), F32),
             pltpu.VMEM((columns // 128, rows), jnp.int32),
             pltpu.VMEM((1, rows), jnp.int32),
             pltpu.VMEM((256, 256), BF16),
             pltpu.VMEM((128, 128), BF16),
             pltpu.VMEM((8, 16, 128), BF16),
-            pltpu.VMEM((c, 2, 4, 2, 4, r, 128), BF16),
-            pltpu.VMEM((c, 4, 2, 4, r, 128), BF16),
-            pltpu.VMEM((c, 2, 4, r, 128), BF16),
-            pltpu.VMEM((c, 2, 4, r, 128), BF16),
-            pltpu.VMEM((c, 2, 2, 4, r, 128), BF16),
-            pltpu.VMEM((c, 2, 2, 4, r, 128), BF16),
-            pltpu.VMEM((c, 3, 2, r, 128), BF16),
-            pltpu.VMEM((c, 2, r, 128), F32),
-            pltpu.VMEM((c, 3, 2, r, 128), BF16),
+            pltpu.VMEM((c, 2, 4, 4, r, 128), BF16),
+            pltpu.VMEM((c, 4, 4, r, 128), BF16),
+            pltpu.VMEM((c, 2, 2, r, 128), BF16),
+            pltpu.VMEM((c, 2, 2, r, 128), BF16),
+            pltpu.VMEM((c, 2, 2, 2, r, 128), BF16),
+            pltpu.VMEM((c, 2, 2, 2, r, 128), BF16),
+            pltpu.VMEM((c, 3, r, 128), BF16),
+            pltpu.VMEM((c, r, 128), F32),
+            pltpu.VMEM((c, 3, r, 128), BF16),
             pltpu.VMEM((2, 8, 16, 128), BF16),
             pltpu.VMEM((16, 16, 128), BF16),
             pltpu.VMEM((8, 16, 128), BF16),

time: 38.5 us -> 39 us (1.013)
  the two profiles are of different devices: /device:TPU:38 before, /device:TPU:64 now
where the time goes in v2:
time: 39 us; the launch traced here: 38.9 us
  Pallas kernels  38.3 us (98%)
  local copies, waits for them, and re-layouts  0.6 us (2%)
    pallas_call x1, Pallas kernels, shards(): pl.pallas_call(kernel, out_shape=jax.ShapeDtypeStruct((16, 128), F32), in...  38.3 us

profile of v2, /device:TPU:64, one launch (start us, length us, event | category | flops | bytes accessed | tf_op | source)
XLA Modules:
  0.0 38.9 jit_solution(4850229191554773405)
XLA Ops:
  0.0 38.3 %reduce_scatter.1 = f32[16,128]{1,0:T(8,128)S(1)} custom-call(f32[128,8192]{1,0:T(8,128)} %bitcast.5, s32[64,128]{1,0:T(8,128)} %bitcast.6, s32[1,128]{1,0:T(1,128)} %bitcast.7), custom_call_target="tpu_custom_call" | custom-call | tf_op jit(solution)/shard_map/reduce_scatter/pallas_call | solution.py:281
  38.3 0.6 %copy.5 = f32[16,128]{1,0:T(8,128)} copy(f32[16,128]{1,0:T(8,128)S(1)} %reduce_scatter.1) | data formatting | bytes 16384

commit v3 on v2

--- a/solution.py
+++ b/solution.py
@@ -14,11 +14,12 @@
 BF16 = jnp.bfloat16
 CHUNKS = 4
 CHUNK_ROWS = 64
+DIRECT = (0, 1)
 ORDER = tuple(
     (item[0], int(item[1:]))
     for line in (
-        "f0 h0 f1 o0", "f2 h1 m0 m1", "h2 k0 m2 f3", "h3 o1 n0 k1", "n1 m3 o2 o3",
-        "k2 n2 k3 r0", "r1 n3 r2 l0", "s0 r3 s1 s2", "s3",
+        "f0 h0 h1 o0", "f1 h2 f2 f3", "k0 h3 n0 k1", "m2 o1 n1 m3", "r0 o2 k2 o3",
+        "n2 k3 r1 n3", "l0 s0 r2 r3", "s1 s2 s3",
     )
     for item in line.split()
 )
@@ -46,7 +47,7 @@
 def kernel(
     grads_ref, first_ref, second_ref, out_ref,
     gbuf, first_buf, second_buf, table, lim1, lim2, enc, arecv,
-    y1send, y1recv, y2send, y2recv, z1send, z1own, z1recv, fsend, frecv, limrecv,
+    y1send, y1recv, y2send, y2recv, z1send, z1own, z1recv, xrecv, fsend, frecv, limrecv,
     load_sem, scale_sem, send_sem, a_rsem, y1_rsem, y2_rsem, z1_rsem, l_rsem, f_rsem,
 ):
     inner = lax.axis_index("inner")
@@ -63,6 +64,7 @@
     sibling = inner_of(y, z, 1 - core)
     right = inner_of(y_right, z, core)
     left = inner_of(y_left, z, core)
+    beside = [inner_of(y_right, z, 1 - core), inner_of(y_left, z, 1 - core)]
     across = inner_of(y, (1 - run) * 4 + role, core)
     mates = [inner_of(y, run * 4 + (role + d) % 4, core) for d in (1, 2, 3)]
 
@@ -124,7 +126,7 @@
             hello(across, outer)
 
     def enter():
-        pl.semaphore_wait(barrier, 21 - 12 * klass)
+        pl.semaphore_wait(barrier, 23 - 12 * klass)
         hello_outer(False)
 
     def enter_outer():
@@ -132,12 +134,11 @@
         def _():
             pl.semaphore_wait(barrier, 12)
 
-    for i in [sibling, right, left] + mates:
+    for i in [sibling, right, left] + beside + mates:
         hello(i, outer)
     hello_outer(True)
 
-    for q in range(1, CHUNKS):
-        start_loads(q)
+    start_loads(1)
     table[...] = sign_table()
     for copy in scale_loads:
         copy.wait()
@@ -155,6 +156,8 @@
         pairs = [(d, k) for d in parts[part] for k in range(4)]
         for d in parts[part]:
             load(q, d).wait()
+        if part == "h" and q + 2 < CHUNKS:
+            start_loads(q + 2)
         lhs = jnp.concatenate(
             [gbuf[q, d, :, k * 256 : (k + 1) * 256].astype(BF16) for d, k in pairs], axis=0
         )
@@ -170,16 +173,26 @@
     def part_copy(q, part):
         span = pl.ds(parts[part][0], len(parts[part]))
         return remote(
-            enc.at[q, 1 - core, span], arecv.at[q, span], 0,
+            enc.at[q, 1 - core, span], arecv.at[q, span], 7 if q in DIRECT else 0,
             a_rsem.at[q, parts[part][0]], sibling,
         )
+
+    def direct_copy(q, way, c):
+        two = pl.ds(2 * way, 2)
+        target = inner_of((y_right, y_left)[way], z, c)
+        return remote(enc.at[q, c, 0, two], xrecv.at[q, core, way], 6, y1_rsem.at[q], target)
 
     def encode_send(part):
         def stage(q):
             encode(q, part)
             if part == "f" and q == 0:
                 enter()
-            part_copy(q, part).start()
+            if part == "f" and q in DIRECT:
+                for way in range(2):
+                    for c in range(2):
+                        direct_copy(q, way, c).start()
+            else:
+                part_copy(q, part).start()
 
         return stage
 
@@ -194,6 +207,8 @@
             remote(lim2.at[owner], limrecv.at[outer], 4, l_rsem.at[0], inner, owner).start()
 
     def ring_far(q):
+        if q in DIRECT:
+            return
         part_copy(q, "f").wait_recv()
         for way, to in ((0, right), (1, left)):
             y1send[q, way] = pair_sum(q, 0, way)
@@ -206,11 +221,15 @@
             remote(y2send.at[q, way, 0], y2recv.at[q, way, 0], 2, y2_rsem.at[q], to).start()
 
     def ring_on(q):
-        wait_recv(y1recv.at[q], y1_rsem.at[q])
+        wait_recv(xrecv.at[q] if q in DIRECT else y1recv.at[q], y1_rsem.at[q])
         for way, to in ((0, right), (1, left)):
             two = pl.ds(2 * way, 2)
             value = enc[q, core, 1 + way, two].astype(F32) + arecv[q, 1 + way, two].astype(F32)
-            y2send[q, way, 1] = (value + y1recv[q, way].astype(F32)).astype(BF16)
+            if q in DIRECT:
+                value = value + xrecv[q, 0, way].astype(F32) + xrecv[q, 1, way].astype(F32)
+            else:
+                value = value + y1recv[q, way].astype(F32)
+            y2send[q, way, 1] = value.astype(BF16)
             remote(y2send.at[q, way, 1], y2recv.at[q, way, 1], 2, y2_rsem.at[q], to).start()
 
     def run_one(q):
@@ -247,6 +266,7 @@
                     inner_of(y, 4 * half + role, core), owner,
                 ).start()
 
+    first_pair, pairs = len(DIRECT), CHUNKS - len(DIRECT)
     stages = {part: encode_send(part) for part in parts}
     stages.update(l=limit_send, m=ring_far, k=ring_near, n=ring_on, r=run_one, s=run_two)
     for name, q in ORDER:
@@ -254,9 +274,12 @@
 
     frecv[8 * run + outer] = fsend[run, outer]
     for stage, like in enumerate(
-        (arecv, y1send, y2send, z1send, lim2.at[pl.ds(0, 7)], frecv.at[pl.ds(0, 15)])
+        (y1send.at[pl.ds(first_pair, pairs)], y2send, z1send, lim2.at[pl.ds(0, 7)], frecv.at[pl.ds(0, 15)])
     ):
-        wait_send(like, stage)
+        wait_send(like, stage + 1)
+    wait_send(xrecv, 6)
+    wait_send(arecv.at[pl.ds(first_pair, pairs)], 0)
+    wait_send(arecv.at[pl.ds(0, len(DIRECT)), pl.ds(1, 3)], 7)
     wait_recv(limrecv.at[pl.ds(0, 7)], l_rsem.at[0])
     wait_recv(frecv.at[pl.ds(0, 15)], f_rsem.at[0])
     total = jnp.zeros((16, 128), F32)
@@ -299,12 +322,13 @@
             pltpu.VMEM((c, 3, r, 128), BF16),
             pltpu.VMEM((c, r, 128), F32),
             pltpu.VMEM((c, 3, r, 128), BF16),
+            pltpu.VMEM((len(DIRECT), 2, 2, 2, r, 128), BF16),
             pltpu.VMEM((2, 8, 16, 128), BF16),
             pltpu.VMEM((16, 16, 128), BF16),
             pltpu.VMEM((8, 16, 128), BF16),
             dma((c, 4)),
             dma((2,)),
-            dma((6,)),
+            dma((8,)),
             dma((c, 4)),
             dma((c,)),
             dma((c,)),

time: 39 us -> 38.4 us (0.985)
  the two profiles are of different devices: /device:TPU:64 before, /device:TPU:384 now
where the time goes in v3:
time: 38.4 us; the launch traced here: 38.2 us
  Pallas kernels  37.6 us (98%)
  local copies, waits for them, and re-layouts  0.6 us (2%)
    pallas_call x1, Pallas kernels, shards(): pl.pallas_call(kernel, out_shape=jax.ShapeDtypeStruct((16, 128), F32), in...  37.6 us

profile of v3, /device:TPU:384, one launch (start us, length us, event | category | flops | bytes accessed | tf_op | source)
XLA Modules:
  0.0 38.2 jit_solution(16947950862428713530)
XLA Ops:
  0.0 37.6 %reduce_scatter.1 = f32[16,128]{1,0:T(8,128)S(1)} custom-call(f32[128,8192]{1,0:T(8,128)} %bitcast.5, s32[64,128]{1,0:T(8,128)} %bitcast.6, s32[1,128]{1,0:T(1,128)} %bitcast.7), custom_call_target="tpu_custom_call" | custom-call | tf_op jit(solution)/shard_map/reduce_scatter/pallas_call | solution.py:304
  37.6 0.6 %copy.5 = f32[16,128]{1,0:T(8,128)} copy(f32[16,128]{1,0:T(8,128)S(1)} %reduce_scatter.1) | data formatting | bytes 16384

commit v4 on v3

--- a/solution.py
+++ b/solution.py
@@ -14,6 +14,7 @@
 BF16 = jnp.bfloat16
 CHUNKS = 4
 CHUNK_ROWS = 64
+HALF = (0, 1, 1, 0)
 DIRECT = (0, 1)
 ORDER = tuple(
     (item[0], int(item[1:]))
@@ -91,7 +92,7 @@
         return pl.ds(q // 2 * CHUNK_ROWS, CHUNK_ROWS)
 
     def load(q, d):
-        columns = pl.ds(pl.multiple_of(places[d] * 2048 + q % 2 * 1024, 1024), 1024)
+        columns = pl.ds(pl.multiple_of(places[d] * 2048 + HALF[q] * 1024, 1024), 1024)
         return pltpu.make_async_copy(
             grads_ref.at[rows_of(q), columns], gbuf.at[q, d], load_sem.at[q, d]
         )
@@ -165,7 +166,7 @@
         rotated = rotated.astype(BF16)
         for i, (d, k) in enumerate(pairs):
             for c in range(2):
-                lane = 16 * d + 8 * (q % 2) + 2 * k + c
+                lane = 16 * d + 8 * HALF[q] + 2 * k + c
                 bound = jnp.broadcast_to(bounds[:, lane : lane + 1], (CHUNK_ROWS, 128))
                 value = rotated[i * CHUNK_ROWS : (i + 1) * CHUNK_ROWS, c * 128 : (c + 1) * 128]
                 enc[q, c, d, k] = clip(value, bound)
@@ -253,7 +254,7 @@
         for d in range(3):
             value = value + z1recv[q, d].astype(F32)
         value = value.astype(BF16)
-        half = q % 2
+        half = HALF[q]
         for h in range(4):
             owner = q // 2 * 4 + h
             fsend[half, owner] = value[h * 16 : (h + 1) * 16]

time: 38.4 us -> 37.8 us (0.984)
  the two profiles are of different devices: /device:TPU:384 before, /device:TPU:416 now
where the time goes in v4:
time: 37.8 us; the launch traced here: 37.7 us
  Pallas kernels  37.1 us (98%)
  local copies, waits for them, and re-layouts  0.6 us (2%)
    pallas_call x1, Pallas kernels, shards(): pl.pallas_call(kernel, out_shape=jax.ShapeDtypeStruct((16, 128), F32), in...  37.1 us

profile of v4, /device:TPU:416, one launch (start us, length us, event | category | flops | bytes accessed | tf_op | source)
XLA Modules:
  0.0 37.7 jit_solution(15506486582104725069)
XLA Ops:
  0.0 37.1 %reduce_scatter.1 = f32[16,128]{1,0:T(8,128)S(1)} custom-call(f32[128,8192]{1,0:T(8,128)} %bitcast.5, s32[64,128]{1,0:T(8,128)} %bitcast.6, s32[1,128]{1,0:T(1,128)} %bitcast.7), custom_call_target="tpu_custom_call" | custom-call | tf_op jit(solution)/shard_map/reduce_scatter/pallas_call | solution.py:305
  37.1 0.6 %copy.5 = f32[16,128]{1,0:T(8,128)} copy(f32[16,128]{1,0:T(8,128)S(1)} %reduce_scatter.1) | data formatting | bytes 16384

commit v5 on v4

--- a/solution.py
+++ b/solution.py
@@ -19,8 +19,8 @@
 ORDER = tuple(
     (item[0], int(item[1:]))
     for line in (
-        "f0 h0 h1 o0", "f1 h2 f2 f3", "k0 h3 n0 k1", "m2 o1 n1 m3", "r0 o2 k2 o3",
-        "n2 k3 r1 n3", "l0 s0 r2 r3", "s1 s2 s3",
+        "f0 h0 h1 o0", "f1 h2 f2 f3", "k0 h3 n0 k1", "m2 o1 n1 m3", "l0 r0 o2 k2",
+        "o3 n2 k3 r1", "n3 s0 r2 r3", "s1 s2 s3",
     )
     for item in line.split()
 )
@@ -128,7 +128,6 @@
 
     def enter():
         pl.semaphore_wait(barrier, 23 - 12 * klass)
-        hello_outer(False)
 
     def enter_outer():
         @pl.when(klass == 1)
@@ -194,6 +193,8 @@
                         direct_copy(q, way, c).start()
             else:
                 part_copy(q, part).start()
+            if part == "f" and q == 0:
+                hello_outer(False)
 
         return stage
 

time: 37.8 us -> 36.5 us (0.966)
  the two profiles are of different devices: /device:TPU:416 before, /device:TPU:480 now
where the time goes in v5:
time: 36.5 us; the launch traced here: 36.3 us
  Pallas kernels  35.7 us (98%)
  local copies, waits for them, and re-layouts  0.6 us (2%)
    pallas_call x1, Pallas kernels, shards(): pl.pallas_call(kernel, out_shape=jax.ShapeDtypeStruct((16, 128), F32), in...  35.7 us

profile of v5, /device:TPU:480, one launch (start us, length us, event | category | flops | bytes accessed | tf_op | source)
XLA Modules:
  0.0 36.3 jit_solution(7330995249763257364)
XLA Ops:
  0.0 35.7 %reduce_scatter.1 = f32[16,128]{1,0:T(8,128)S(1)} custom-call(f32[128,8192]{1,0:T(8,128)} %bitcast.5, s32[64,128]{1,0:T(8,128)} %bitcast.6, s32[1,128]{1,0:T(1,128)} %bitcast.7), custom_call_target="tpu_custom_call" | custom-call | tf_op jit(solution)/shard_map/reduce_scatter/pallas_call | solution.py:306
  35.7 0.6 %copy.5 = f32[16,128]{1,0:T(8,128)} copy(f32[16,128]{1,0:T(8,128)S(1)} %reduce_scatter.1) | data formatting | bytes 16384

commit v6 on v4

--- a/solution.py
+++ b/solution.py
@@ -19,8 +19,8 @@
 ORDER = tuple(
     (item[0], int(item[1:]))
     for line in (
-        "f0 h0 h1 o0", "f1 h2 f2 f3", "k0 h3 n0 k1", "m2 o1 n1 m3", "r0 o2 k2 o3",
-        "n2 k3 r1 n3", "l0 s0 r2 r3", "s1 s2 s3",
+        "f0 h0 h1 o0", "f1 h2 f2 f3", "p0 k0 h3 n0", "k1 m2 o1 n1", "m3 l0 r0 o2",
+        "k2 o3 n2 k3", "r1 n3 s0 r2", "r3 s1 s2 s3",
     )
     for item in line.split()
 )
@@ -112,32 +112,42 @@
     def hello(i, o):
         pl.semaphore_signal(barrier, inc=1, device_id=(i, o), device_id_type=LOGICAL)
 
-    def hello_outer(same):
-        for d in range(1, 8):
-            owner = (outer + d) % 8
-            other_lower = 1 - owner // 4
-            for i, other in ((inner, other_lower * first_run), (across, other_lower * run)):
-
-                @pl.when((other == klass) if same else (other != klass))
-                def _():
-                    hello(i, owner)
-
-        @pl.when((lower * run == klass) if same else (lower * run != klass))
+    def hello_first():
+        for i in [sibling, right, left] + beside + mates:
+            hello(i, outer)
+        for d in range(1, 4):
+            hello(inner, outer // 4 * 4 + (outer + d) % 4)
+
+        @pl.when(klass == 0)
         def _():
-            hello(across, outer)
+            other = lower * inner + (1 - lower) * (first_run * across + run * inner)
+            for j in range(4):
+                hello(across, 4 + j)
+                hello(other, 4 * lower + j)
+
+    def hello_second(q):
+        @pl.when(klass == 1)
+        def _():
+            for j in range(4):
+                hello(across, j)
+                hello(across, 4 + j)
+                hello(inner, 4 + j)
+
+        @pl.when(klass == 0)
+        def _():
+            early = lower * across + (1 - lower) * (first_run * inner + run * across)
+            for j in range(4):
+                hello(early, j)
 
     def enter():
         pl.semaphore_wait(barrier, 23 - 12 * klass)
-        hello_outer(False)
 
     def enter_outer():
         @pl.when(klass == 1)
         def _():
             pl.semaphore_wait(barrier, 12)
 
-    for i in [sibling, right, left] + beside + mates:
-        hello(i, outer)
-    hello_outer(True)
+    hello_first()
 
     start_loads(1)
     table[...] = sign_table()
@@ -269,7 +279,7 @@
 
     first_pair, pairs = len(DIRECT), CHUNKS - len(DIRECT)
     stages = {part: encode_send(part) for part in parts}
-    stages.update(l=limit_send, m=ring_far, k=ring_near, n=ring_on, r=run_one, s=run_two)
+    stages.update(p=hello_second, l=limit_send, m=ring_far, k=ring_near, n=ring_on, r=run_one, s=run_two)
     for name, q in ORDER:
         stages[name](q)
 

time: 37.8 us -> 36.8 us (0.974)
  the two profiles are of different devices: /device:TPU:416 before, /device:TPU:480 now
where the time goes in v6:
time: 36.8 us; the launch traced here: 36.6 us
  Pallas kernels  36 us (98%)
  local copies, waits for them, and re-layouts  0.6 us (2%)
    pallas_call x1, Pallas kernels, shards(): pl.pallas_call(kernel, out_shape=jax.ShapeDtypeStruct((16, 128), F32), in...  36 us

profile of v6, /device:TPU:480, one launch (start us, length us, event | category | flops | bytes accessed | tf_op | source)
XLA Modules:
  0.0 36.6 jit_solution(10880100299388921376)
XLA Ops:
  0.0 36.0 %reduce_scatter.1 = f32[16,128]{1,0:T(8,128)S(1)} custom-call(f32[128,8192]{1,0:T(8,128)} %bitcast.5, s32[64,128]{1,0:T(8,128)} %bitcast.6, s32[1,128]{1,0:T(1,128)} %bitcast.7), custom_call_target="tpu_custom_call" | custom-call | tf_op jit(solution)/shard_map/reduce_scatter/pallas_call | solution.py:315
  36.0 0.6 %copy.5 = f32[16,128]{1,0:T(8,128)} copy(f32[16,128]{1,0:T(8,128)S(1)} %reduce_scatter.1) | data formatting | bytes 16384

commit v7 on v6

--- a/solution.py
+++ b/solution.py
@@ -19,8 +19,8 @@
 ORDER = tuple(
     (item[0], int(item[1:]))
     for line in (
-        "f0 h0 h1 o0", "f1 h2 f2 f3", "p0 k0 h3 n0", "k1 m2 o1 n1", "m3 l0 r0 o2",
-        "k2 o3 n2 k3", "r1 n3 s0 r2", "r3 s1 s2 s3",
+        "f0 h0 o0 h1", "f1 h2 f2 f3", "p0 k0 h3 n0", "k1 m2 n1 m3", "l0 r0 k2 n2",
+        "k3 r1 n3 s0", "r2 r3 s1 s2", "s3",
     )
     for item in line.split()
 )
@@ -86,7 +86,9 @@
         pltpu.make_async_copy(second_ref, second_buf, scale_sem.at[1]),
     ]
     places = (y_far, y_right, y_left, y)
-    parts = {"f": (0,), "h": (1, 2), "o": (3,)}
+
+    def places_of(q, part):
+        return {"f": (0,), "h": (1, 2, 3) if q else (1, 2), "o": (3,)}[part]
 
     def rows_of(q):
         return pl.ds(q // 2 * CHUNK_ROWS, CHUNK_ROWS)
@@ -126,6 +128,11 @@
                 hello(other, 4 * lower + j)
 
     def hello_second(q):
+        second = jnp.broadcast_to(limits(second_buf[...]), (128, 128)).T.astype(BF16)
+        for owner in range(8):
+            lim2[owner] = second[owner * 16 : (owner + 1) * 16]
+        limrecv[outer] = lim2[outer]
+
         @pl.when(klass == 1)
         def _():
             for j in range(4):
@@ -149,7 +156,6 @@
 
     hello_first()
 
-    start_loads(1)
     table[...] = sign_table()
     for copy in scale_loads:
         copy.wait()
@@ -157,15 +163,11 @@
         [first_buf[pl.ds(pl.multiple_of(place * 16, 16), 16), :] for place in places] * 2, axis=0
     )
     lim1[...] = limits(first).T.astype(BF16)
-    second = jnp.broadcast_to(limits(second_buf[...]), (128, 128)).T.astype(BF16)
-    for owner in range(8):
-        lim2[owner] = second[owner * 16 : (owner + 1) * 16]
-    limrecv[outer] = lim2[outer]
 
     def encode(q, part):
         bounds = lim1[rows_of(q), :]
-        pairs = [(d, k) for d in parts[part] for k in range(4)]
-        for d in parts[part]:
+        pairs = [(d, k) for d in places_of(q, part) for k in range(4)]
+        for d in places_of(q, part):
             load(q, d).wait()
         if part == "h" and q + 2 < CHUNKS:
             start_loads(q + 2)
@@ -182,10 +184,11 @@
                 enc[q, c, d, k] = clip(value, bound)
 
     def part_copy(q, part):
-        span = pl.ds(parts[part][0], len(parts[part]))
+        places = places_of(q, part)
+        span = pl.ds(places[0], len(places))
         return remote(
             enc.at[q, 1 - core, span], arecv.at[q, span], 7 if q in DIRECT else 0,
-            a_rsem.at[q, parts[part][0]], sibling,
+            a_rsem.at[q, places[0]], sibling,
         )
 
     def direct_copy(q, way, c):
@@ -204,6 +207,8 @@
                         direct_copy(q, way, c).start()
             else:
                 part_copy(q, part).start()
+            if part == "f" and q == 0:
+                start_loads(1)
 
         return stage
 
@@ -244,7 +249,8 @@
             remote(y2send.at[q, way, 1], y2recv.at[q, way, 1], 2, y2_rsem.at[q], to).start()
 
     def run_one(q):
-        part_copy(q, "o").wait_recv()
+        if q == 0:
+            part_copy(q, "o").wait_recv()
         wait_recv(y2recv.at[q], y2_rsem.at[q])
         for d in (1, 2, 3, 0):
             r = (role + d) % 4
@@ -278,7 +284,7 @@
                 ).start()
 
     first_pair, pairs = len(DIRECT), CHUNKS - len(DIRECT)
-    stages = {part: encode_send(part) for part in parts}
+    stages = {part: encode_send(part) for part in "fho"}
     stages.update(p=hello_second, l=limit_send, m=ring_far, k=ring_near, n=ring_on, r=run_one, s=run_two)
     for name, q in ORDER:
         stages[name](q)

time: 36.8 us -> 37.9 us (1.030)
  the two profiles are of different devices: /device:TPU:480 before, /device:TPU:352 now
where the time goes in v7:
time: 37.9 us; the launch traced here: 37.7 us
  Pallas kernels  37.1 us (98%)
  local copies, waits for them, and re-layouts  0.6 us (2%)
    pallas_call x1, Pallas kernels, shards(): pl.pallas_call(kernel, out_shape=jax.ShapeDtypeStruct((16, 128), F32), in...  37.1 us

profile of v7, /device:TPU:352, one launch (start us, length us, event | category | flops | bytes accessed | tf_op | source)
XLA Modules:
  0.0 37.7 jit_solution(14862449440284517949)
XLA Ops:
  0.0 37.1 %reduce_scatter.1 = f32[16,128]{1,0:T(8,128)S(1)} custom-call(f32[128,8192]{1,0:T(8,128)} %bitcast.5, s32[64,128]{1,0:T(8,128)} %bitcast.6, s32[1,128]{1,0:T(1,128)} %bitcast.7), custom_call_target="tpu_custom_call" | custom-call | tf_op jit(solution)/shard_map/reduce_scatter/pallas_call | solution.py:321
  37.1 0.6 %copy.5 = f32[16,128]{1,0:T(8,128)} copy(f32[16,128]{1,0:T(8,128)S(1)} %reduce_scatter.1) | data formatting | bytes 16384

commit v8 on v6

--- a/solution.py
+++ b/solution.py
@@ -103,7 +103,7 @@
 
     for copy in scale_loads:
         copy.start()
-    start_loads(0)
+    load(0, 0).start()
 
     lower, first_run = 1 - outer // 4, 1 - run
     klass = lower * first_run
@@ -148,6 +148,8 @@
             pl.semaphore_wait(barrier, 12)
 
     hello_first()
+    for d in (1, 2, 3):
+        load(0, d).start()
 
     start_loads(1)
     table[...] = sign_table()
@@ -157,10 +159,6 @@
         [first_buf[pl.ds(pl.multiple_of(place * 16, 16), 16), :] for place in places] * 2, axis=0
     )
     lim1[...] = limits(first).T.astype(BF16)
-    second = jnp.broadcast_to(limits(second_buf[...]), (128, 128)).T.astype(BF16)
-    for owner in range(8):
-        lim2[owner] = second[owner * 16 : (owner + 1) * 16]
-    limrecv[outer] = lim2[outer]
 
     def encode(q, part):
         bounds = lim1[rows_of(q), :]
@@ -212,6 +210,10 @@
         return enc[q, core, d, two] + arecv[q, d, two]
 
     def limit_send(q):
+        second = jnp.broadcast_to(limits(second_buf[...]), (128, 128)).T.astype(BF16)
+        for owner in range(8):
+            lim2[owner] = second[owner * 16 : (owner + 1) * 16]
+        limrecv[outer] = lim2[outer]
         enter_outer()
         for d in range(1, 8):
             owner = (outer + d) % 8

time: 36.8 us -> 36.7 us (level)
  no operation moved by 1% of the time
where the time goes in v8:
time: 36.7 us; the launch traced here: 36.5 us
  Pallas kernels  35.9 us (98%)
  local copies, waits for them, and re-layouts  0.6 us (2%)
    pallas_call x1, Pallas kernels, shards(): pl.pallas_call(kernel, out_shape=jax.ShapeDtypeStruct((16, 128), F32), in...  35.9 us

profile of v8, /device:TPU:480, one launch (start us, length us, event | category | flops | bytes accessed | tf_op | source)
XLA Modules:
  0.0 36.5 jit_solution(9745664119106647544)
XLA Ops:
  0.0 35.9 %reduce_scatter.1 = f32[16,128]{1,0:T(8,128)S(1)} custom-call(f32[128,8192]{1,0:T(8,128)} %bitcast.5, s32[64,128]{1,0:T(8,128)} %bitcast.6, s32[1,128]{1,0:T(1,128)} %bitcast.7), custom_call_target="tpu_custom_call" | custom-call | tf_op jit(solution)/shard_map/reduce_scatter/pallas_call | solution.py:317
  35.9 0.6 %copy.5 = f32[16,128]{1,0:T(8,128)} copy(f32[16,128]{1,0:T(8,128)S(1)} %reduce_scatter.1) | data formatting | bytes 16384

commit v9 on v8

--- a/solution.py
+++ b/solution.py
@@ -19,7 +19,7 @@
 ORDER = tuple(
     (item[0], int(item[1:]))
     for line in (
-        "f0 h0 h1 o0", "f1 h2 f2 f3", "p0 k0 h3 n0", "k1 m2 o1 n1", "m3 l0 r0 o2",
+        "f0 h0 h1 f1", "h2 f2 f3 p0", "k0 n0 o0 h3", "k1 m2 o1 n1", "m3 l0 r0 o2",
         "k2 o3 n2 k3", "r1 n3 s0 r2", "r3 s1 s2 s3",
     )
     for item in line.split()

time: 36.7 us -> 36.7 us (level)
  no operation moved by 1% of the time
where the time goes in v9:
time: 36.7 us; the launch traced here: 36.4 us
  Pallas kernels  35.8 us (98%)
  local copies, waits for them, and re-layouts  0.6 us (2%)
    pallas_call x1, Pallas kernels, shards(): pl.pallas_call(kernel, out_shape=jax.ShapeDtypeStruct((16, 128), F32), in...  35.8 us

profile of v9, /device:TPU:480, one launch (start us, length us, event | category | flops | bytes accessed | tf_op | source)
XLA Modules:
  0.0 36.4 jit_solution(6009287057187788394)
XLA Ops:
  0.0 35.8 %reduce_scatter.1 = f32[16,128]{1,0:T(8,128)S(1)} custom-call(f32[128,8192]{1,0:T(8,128)} %bitcast.5, s32[64,128]{1,0:T(8,128)} %bitcast.6, s32[1,128]{1,0:T(1,128)} %bitcast.7), custom_call_target="tpu_custom_call" | custom-call | tf_op jit(solution)/shard_map/reduce_scatter/pallas_call | solution.py:317
  35.8 0.6 %copy.5 = f32[16,128]{1,0:T(8,128)} copy(f32[16,128]{1,0:T(8,128)S(1)} %reduce_scatter.1) | data formatting | bytes 16384

commit v10 on v9

--- a/solution.py
+++ b/solution.py
@@ -229,9 +229,8 @@
 
     def ring_near(q):
         part_copy(q, "h").wait_recv()
-        for way, to in ((0, right), (1, left)):
+        for way in range(2):
             y2send[q, way, 0] = pair_sum(q, 1 + way, 1 - way)
-            remote(y2send.at[q, way, 0], y2recv.at[q, way, 0], 2, y2_rsem.at[q], to).start()
 
     def ring_on(q):
         wait_recv(xrecv.at[q] if q in DIRECT else y1recv.at[q], y1_rsem.at[q])
@@ -243,7 +242,7 @@
             else:
                 value = value + y1recv[q, way].astype(F32)
             y2send[q, way, 1] = value.astype(BF16)
-            remote(y2send.at[q, way, 1], y2recv.at[q, way, 1], 2, y2_rsem.at[q], to).start()
+            remote(y2send.at[q, way], y2recv.at[q, way], 2, y2_rsem.at[q], to).start()
 
     def run_one(q):
         part_copy(q, "o").wait_recv()
@@ -267,17 +266,24 @@
             value = value + z1recv[q, d].astype(F32)
         value = value.astype(BF16)
         half = HALF[q]
+        band = q // 2
         for h in range(4):
-            owner = q // 2 * 4 + h
-            fsend[half, owner] = value[h * 16 : (h + 1) * 16]
-            here = jnp.logical_and(owner == outer, half == run)
-
-            @pl.when(jnp.logical_not(here))
-            def _():
-                remote(
-                    fsend.at[half, owner], frecv.at[8 * run + outer], 5, f_rsem.at[0],
-                    inner_of(y, 4 * half + role, core), owner,
-                ).start()
+            fsend[half, band * 4 + h] = value[h * 16 : (h + 1) * 16]
+
+        def owner_copy(h):
+            owner = band * 4 + (outer + h) % 4
+            return remote(
+                fsend.at[half, owner], frecv.at[8 * run + outer], 5, f_rsem.at[0],
+                inner_of(y, 4 * half + role, core), owner,
+            )
+
+        for h in range(1, 4):
+            owner_copy(h).start()
+        here = jnp.logical_and(outer // 4 == band, half == run)
+
+        @pl.when(jnp.logical_not(here))
+        def _():
+            owner_copy(0).start()
 
     first_pair, pairs = len(DIRECT), CHUNKS - len(DIRECT)
     stages = {part: encode_send(part) for part in parts}

time: 36.7 us -> 37.3 us (1.016)
  Pallas kernels: 35.8 us -> 36.3 us
    pallas_call x1, Pallas kernels: 35.8 us -> 36.3 us  [shards(): pl.pallas_call(kernel, out_shape=jax.ShapeDtypeStruct((16, 128), F32), in...]
where the time goes in v10:
time: 37.3 us; the launch traced here: 36.9 us
  Pallas kernels  36.3 us (97%)
  local copies, waits for them, and re-layouts  0.6 us (2%)
    pallas_call x1, Pallas kernels, shards(): pl.pallas_call(kernel, out_shape=jax.ShapeDtypeStruct((16, 128), F32), in...  36.3 us

profile of v10, /device:TPU:480, one launch (start us, length us, event | category | flops | bytes accessed | tf_op | source)
XLA Modules:
  0.0 36.9 jit_solution(6667174425720649304)
XLA Ops:
  0.0 36.3 %reduce_scatter.1 = f32[16,128]{1,0:T(8,128)S(1)} custom-call(f32[128,8192]{1,0:T(8,128)} %bitcast.5, s32[64,128]{1,0:T(8,128)} %bitcast.6, s32[1,128]{1,0:T(1,128)} %bitcast.7), custom_call_target="tpu_custom_call" | custom-call | tf_op jit(solution)/shard_map/reduce_scatter/pallas_call | solution.py:323
  36.3 0.6 %copy.5 = f32[16,128]{1,0:T(8,128)} copy(f32[16,128]{1,0:T(8,128)S(1)} %reduce_scatter.1) | data formatting | bytes 16384

commit v11 on v10

--- a/solution.py
+++ b/solution.py
@@ -19,7 +19,7 @@
 ORDER = tuple(
     (item[0], int(item[1:]))
     for line in (
-        "f0 h0 h1 f1", "h2 f2 f3 p0", "k0 n0 o0 h3", "k1 m2 o1 n1", "m3 l0 r0 o2",
+        "f0 h0 h1 f1", "h2 f2 f3 p0", "k0 n0 o0 h3", "k1 m2 o1 n1", "m3 r0 l0 o2",
         "k2 o3 n2 k3", "r1 n3 s0 r2", "r3 s1 s2 s3",
     )
     for item in line.split()
@@ -229,8 +229,9 @@
 
     def ring_near(q):
         part_copy(q, "h").wait_recv()
-        for way in range(2):
+        for way, to in ((0, right), (1, left)):
             y2send[q, way, 0] = pair_sum(q, 1 + way, 1 - way)
+            remote(y2send.at[q, way, 0], y2recv.at[q, way, 0], 2, y2_rsem.at[q], to).start()
 
     def ring_on(q):
         wait_recv(xrecv.at[q] if q in DIRECT else y1recv.at[q], y1_rsem.at[q])
@@ -242,7 +243,7 @@
             else:
                 value = value + y1recv[q, way].astype(F32)
             y2send[q, way, 1] = value.astype(BF16)
-            remote(y2send.at[q, way], y2recv.at[q, way], 2, y2_rsem.at[q], to).start()
+            remote(y2send.at[q, way, 1], y2recv.at[q, way, 1], 2, y2_rsem.at[q], to).start()
 
     def run_one(q):
         part_copy(q, "o").wait_recv()

time: 37.3 us -> 36.7 us (0.984)
  Pallas kernels: 36.3 us -> 35.9 us
where the time goes in v11:
time: 36.7 us; the launch traced here: 36.5 us
  Pallas kernels  35.9 us (98%)
  local copies, waits for them, and re-layouts  0.6 us (2%)
    pallas_call x1, Pallas kernels, shards(): pl.pallas_call(kernel, out_shape=jax.ShapeDtypeStruct((16, 128), F32), in...  35.9 us

profile of v11, /device:TPU:480, one launch (start us, length us, event | category | flops | bytes accessed | tf_op | source)
XLA Modules:
  0.0 36.5 jit_solution(10597449385337791350)
XLA Ops:
  0.0 35.9 %reduce_scatter.1 = f32[16,128]{1,0:T(8,128)S(1)} custom-call(f32[128,8192]{1,0:T(8,128)} %bitcast.5, s32[64,128]{1,0:T(8,128)} %bitcast.6, s32[1,128]{1,0:T(1,128)} %bitcast.7), custom_call_target="tpu_custom_call" | custom-call | tf_op jit(solution)/shard_map/reduce_scatter/pallas_call | solution.py:324
  35.9 0.6 %copy.5 = f32[16,128]{1,0:T(8,128)} copy(f32[16,128]{1,0:T(8,128)S(1)} %reduce_scatter.1) | data formatting | bytes 16384
